TPU v7x, 512 devices: a whole 4x8x8 slice. The times are simulated.
512 devices in a mesh: prow: 32 (over z, x), pcol: 16 (over y, core).
Axes of the slice: x: 4, y: 8, z: 8, core: 2. Of those that a mesh axis runs over, the one named last changes fastest.
Arguments:
- trailing: float32 [16384, 16384], P('prow', 'pcol'), may hold values from -48 to 48, as said below
- panel: float32 [16384, 256], P('prow', 'pcol'), may hold values from -48 to 48, as said below
Outputs:
- updated: float32 [16384, 16384], P('prow', 'pcol')
- basis_out: float32 [16384, 256], P('prow')
Inputs may be any that keep to these rules, and one draw needn't show every extreme that they name: trailing is exactly symmetric, with a positive added diagonal. panel has full column rank.
All inputs are finite; a program needn't handle non-finite values.
Results may differ from a plain program's by a relative error of at most 0.000096.
Values sent between devices are 32-bit elements; how exact they have to be, the bound alone decides.
No kernel may reach another device: no remote copies, remote signals or barrier semaphores. Data moves between devices by JAX's collectives and lax.ppermute only.
A program may use at most 64 MiB of HBM per device.

v0:
```python
import jax
import jax.numpy as jnp
from jax import lax
from jax.sharding import PartitionSpec as P


def spread(value, axis, source):
    kept = jnp.where(lax.axis_index(axis) == source, value, 0).astype(value.dtype)
    return lax.psum(kept, axis)


def matmul(left, right):
    return jnp.dot(left, right, precision=lax.Precision.HIGHEST, preferred_element_type=jnp.float32)


def shards(trailing, panel):
    fanout_count = lax.axis_size("prow") // lax.axis_size("pcol")
    column_index = lax.axis_index("pcol")
    panel_rows = lax.all_gather(panel, "pcol", axis=1, tiled=True)
    gram_total = lax.psum(matmul(panel_rows.T, panel_rows), "prow")
    factor = jnp.linalg.cholesky(gram_total)
    basis_rows = lax.linalg.triangular_solve(
        factor, panel_rows, left_side=False, lower=True, transpose_a=True
    )
    basis_cols = jnp.concatenate(
        [
            spread(basis_rows, "prow", column_index * fanout_count + offset)
            for offset in range(fanout_count)
        ],
        0,
    )
    product = lax.psum(matmul(trailing, basis_cols), "pcol")
    projected = lax.psum(matmul(basis_rows.T, product), "prow")
    correction = product - 0.5 * matmul(basis_rows, projected)
    correction_cols = jnp.concatenate(
        [
            spread(correction, "prow", column_index * fanout_count + offset)
            for offset in range(fanout_count)
        ],
        0,
    )
    updated = trailing - matmul(basis_rows, correction_cols.T) - matmul(correction, basis_cols.T)
    return (updated, basis_rows)


def solution(mesh):
    in_specs = (P("prow", "pcol"), P("prow", "pcol"))
    out_specs = (P("prow", "pcol"), P("prow", None))
    return jax.shard_map(shards, mesh=mesh, in_specs=in_specs, out_specs=out_specs, check_vma=False)
```

profile of v0, /device:TPU:1, one launch (start us, length us, event | category | flops | bytes accessed | tf_op | source)
XLA Modules:
  0.0 858.0 jit_solution(2301283968805448627)
XLA Ops:
  7.2 0.0 all-reduce.9.cloned.1.call-start
  7.2 22.7 %all_gather.3 = f32[512,256]{0,1:T(8,128)S(1)} all-gather(f32[512,16]{0,1:T(8,128)} %param.3), channel_id=1, replica_groups=mesh['prow'=32,'pcol'=16] {'pcol'}, dimensions={1}, use_global_device_ids=true | all-gather | bytes 557056 | tf_op jit(solution)/shard_map/all_gather | solution.py:19
  29.9 1.3 fusion.16
  31.2 0.0 all-reduce.9.cloned.1.call-update
  31.2 0.0 all-reduce.17.cloned.1.call-start
  31.3 150.4 %all-reduce.9.cloned.1.call-done = f32[256,256]{0,1:T(8,128)} async-done(((f32[256,256]{0,1:T(8,128)}), f32[256,256]{0,1:T(8,128)}) %all-reduce.9.cloned.1.call-update) | async-done | bytes 262160 | tf_op jit(solution)/shard_map/psum | solution.py:20
  181.8 1.1 copy.5
  182.9 1.0 fusion.7
  183.9 11.7 %cholesky.50 = f32[128,128]{1,0:T(8,128)S(1)} custom-call(f32[128,128]{1,0:T(8,128)S(1)} %cholesky.118), custom_call_target="Cholesky" | custom-call | tf_op jit(solution)/shard_map/jit(cholesky)/cholesky | solution.py:21
  195.6 9.8 %custom-call.14 = f32[1,128,128]{1,2,0:T(8,128)S(1)} custom-call(f32[1,128,128]{2,1,0:T(8,128)S(1)} %get-tuple-element.34), custom_call_target="InvertDiagBlocksLowerTriangular" | custom-call | tf_op jit(solution)/shard_map/jit(cholesky)/cholesky | solution.py:21
  205.5 0.2 constant_dynamic-update-slice_fusion.3
  205.7 0.3 convolution_subtract_fusion.1
  205.9 11.7 %cholesky.105 = f32[128,128]{1,0:T(8,128)S(1)} custom-call(f32[128,128]{1,0:T(8,128)S(1)} %convolution_subtract_fusion.1), custom_call_target="Cholesky" | custom-call | tf_op jit(solution)/shard_map/jit(cholesky)/cholesky | solution.py:21
  217.7 0.7 compare_reduce_fusion
  219.7 0.1 triangular_solve.59
  219.8 4.1 while.1
  219.9 0.6 fusion.30
  220.5 1.4 bitcast_dynamic-update-slice_fusion.2
  221.9 0.6 fusion.30
  222.5 1.4 bitcast_dynamic-update-slice_fusion.2
  223.9 19.7 %custom-call.15 = f32[2,128,128]{1,2,0:T(8,128)S(1)} custom-call(f32[2,128,128]{2,1,0:T(8,128)S(1)} %get-tuple-element.9), custom_call_target="InvertDiagBlocksLowerTriangular" | custom-call | tf_op jit(solution)/shard_map/triangular_solve | solution.py:22
  243.6 0.4 fusion.5
  244.0 0.4 convolution_subtract_fusion
  244.4 1.1 fusion.8
  245.5 2.3 pad_maximum_fusion
  247.8 0.0 copy-start
  247.8 0.0 all-reduce.17.cloned.1.call-update
  247.8 0.0 all-reduce.11.cloned.1.call-start
  247.9 157.8 %all-reduce.17.cloned.1.call-done = (f32[512,256]{0,1:T(8,128)}, f32[512,256]{0,1:T(8,128)}) async-done(((f32[512,256]{0,1:T(8,128)}, f32[512,256]{0,1:T(8,128)}), (f32[512,256]{0,1:T(8,128)}, f32[512,256]{0,1:T(8,128)})) %all-reduce.17.cloned.1.call-update) | async-done | bytes 1048592 | tf_op jit(solution)/shard_map/psum | solution.py:9
  405.6 1.1 constant_dynamic-update-slice_fusion.1
  406.7 1.1 constant_dynamic-update-slice_fusion
  407.8 0.0 copy-done
  407.8 2.7 convolution_bitcast_fusion
  410.5 0.0 all-reduce.11.cloned.1.call-update
  410.5 0.0 all-reduce.13.cloned.1.call-start
  410.6 116.5 %all-reduce.11.cloned.1.call-done = f32[512,256]{0,1:T(8,128)} async-done(((f32[512,256]{0,1:T(8,128)}), f32[512,256]{0,1:T(8,128)}) %all-reduce.11.cloned.1.call-update) | async-done | bytes 524304 | tf_op jit(solution)/shard_map/psum | solution.py:32
  527.1 2.4 fusion.14
  529.6 0.0 all-reduce.13.cloned.1.call-update
  529.6 0.0 all-reduce.15.cloned.1.call-start
  529.6 153.7 %all-reduce.13.cloned.1.call-done = f32[256,256]{1,0:T(8,128)} async-done(((f32[256,256]{1,0:T(8,128)}), f32[256,256]{1,0:T(8,128)}) %all-reduce.13.cloned.1.call-update) | async-done | bytes 262160 | tf_op jit(solution)/shard_map/psum | solution.py:33
  683.3 3.1 broadcast_select_fusion.1
  686.4 0.0 all-reduce.15.cloned.1.call-update
  686.4 2.0 copy.7
  688.4 156.4 %all-reduce.15.cloned.1.call-done = (f32[512,256]{0,1:T(8,128)}, f32[512,256]{0,1:T(8,128)}) async-done(((f32[512,256]{0,1:T(8,128)}, f32[512,256]{0,1:T(8,128)}), (f32[512,256]{0,1:T(8,128)}, f32[512,256]{0,1:T(8,128)})) %all-reduce.15.cloned.1.call-update) | async-done | bytes 1048592 | tf_op jit(solution)/shard_map/psum | solution.py:9
  844.8 0.0 copy-start.1
  844.8 3.2 fusion.1
  848.0 0.0 copy-done.1
  848.0 3.4 subtract_subtract_fusion
  (9 shorter events, 0.1 us)
Async XLA Ops:
  7.2 174.6 %all-reduce.9.cloned.1.call-start = ((), (), s32[]{:S(2)}) async-start(), calls=%async_computation | async-start | bytes 524288 | tf_op jit(solution)/shard_map/psum | solution.py:20
  31.2 374.4 %all-reduce.17.cloned.1.call-start = ((), (), s32[]{:S(2)}) async-start(), calls=%async_computation.4 | async-start | bytes 2097152 | tf_op jit(solution)/shard_map/psum | solution.py:9
  247.8 160.0 %copy-start = (f32[512,1024]{1,0:T(8,128)S(1)}, f32[512,1024]{1,0:T(8,128)}, u32[]{:S(2)}) copy-start(f32[512,1024]{1,0:T(8,128)} %param.2) | copy-start | bytes 6291460
  247.8 279.3 %all-reduce.11.cloned.1.call-start = ((), (), s32[]{:S(2)}) async-start(), calls=%async_computation.1 | async-start | bytes 1048576 | tf_op jit(solution)/shard_map/psum | solution.py:32
  410.5 272.7 %all-reduce.13.cloned.1.call-start = ((), (), s32[]{:S(2)}) async-start(), calls=%async_computation.2 | async-start | bytes 524288 | tf_op jit(solution)/shard_map/psum | solution.py:33
  529.6 315.2 %all-reduce.15.cloned.1.call-start = ((), (), s32[]{:S(2)}) async-start(), calls=%async_computation.3 | async-start | bytes 2097152 | tf_op jit(solution)/shard_map/psum | solution.py:9
  844.8 3.2 copy-start.1
Sparse Core Ops, SparseCore 0:
  31.4 150.3 all-reduce.8
  247.9 157.6 all-reduce.16
  410.7 116.3 all-reduce.10
  531.4 151.8 all-reduce.12
  687.1 157.6 all-reduce.14
where the time goes:
time: 862 us; the launch traced here: 858 us
  waiting for transfers between devices  735 us (85%)
  other arithmetic  57 us (7%)
  blocking collectives  22.7 us (3%)
  matrix products  18.6 us (2%)
  between operations  15.2 us (2%)
  local copies, waits for them, and re-layouts  9.3 us (1%)
    psum x2, waiting for transfers between devices, spread(): return lax.psum(kept, axis)  314 us
    psum x1, waiting for transfers between devices, shards(): projected = lax.psum(matmul(basis_rows.T, product), 'prow')  154 us
    psum x1, waiting for transfers between devices, shards(): gram_total = lax.psum(matmul(panel_rows.T, panel_rows), 'prow')  150 us
    psum x1, waiting for transfers between devices, shards(): product = lax.psum(matmul(trailing, basis_cols), 'pcol')  117 us
    another operation x6, other arithmetic, shards(): factor = jnp.linalg.cholesky(gram_total)  34 us
    all_gather x1, blocking collectives, shards(): panel_rows = lax.all_gather(panel, 'pcol', axis=1, tiled=True)  22.7 us
    another operation x4, other arithmetic, shards(): lax.linalg.triangular_solve(factor, panel_rows, left_side=False, lower=Tr...  22 us
  transfers between devices with their start and end apart: 5, of which 5 were waited for; matrix products, arithmetic and copies ran while one was open for 0% of the time, Pallas kernels for 0%

commit v1 on v0

v1 whole, which is shorter than its diff:
```python
import jax
import jax.numpy as jnp
from jax import lax
from jax.sharding import Mesh, PartitionSpec as P

ROWS = ("z", "x")
COLS = ("y", "c")
ALL = ("z", "x", "y", "c")
BLOCK = 32


def matmul(left, right, contract, precision=lax.Precision.HIGHEST):
    return lax.dot_general(
        left, right, ((contract[:1], contract[1:]), ((), ())),
        precision=precision, preferred_element_type=jnp.float32,
    )


def exchange(value, axis):
    return lax.all_to_all(value, axis, 0, 0, tiled=True)


def repeat(value, count):
    return jnp.broadcast_to(value[None], (count, *value.shape))


def blocks_of_columns():
    pairs = []
    for z in range(8):
        for x in range(4):
            for col in range(16):
                part = 8 * x + z
                row = 2 * col + part // 16
                pairs.append((row * 16 + part % 16, (z * 4 + x) * 16 + col))
    return pairs


def shards(trailing, panel):
    order = panel.shape[0] // BLOCK
    width = panel.shape[1] * order
    column = lax.axis_index(COLS)
    pairs = blocks_of_columns()
    high = lax.Precision.HIGH

    panel_rows = lax.all_gather(panel, COLS, axis=1, tiled=True)
    block = lax.dynamic_slice(panel_rows, (column * BLOCK, 0), (BLOCK, width))
    panel_block = lax.ppermute(block, ALL, pairs)

    partial = matmul(trailing, panel_rows, (0, 0), high)
    partial = lax.optimization_barrier((partial, panel_block))[0]
    partial = exchange(partial.reshape(4, 256, width), "x").sum(0)
    product_block = exchange(partial.reshape(8, BLOCK, width), "z").sum(0)

    both = jnp.concatenate([product_block, panel_block], 1)
    both = exchange(repeat(both, 8), "z").reshape(256, 2 * width)
    both_cols = exchange(repeat(both, 4), "x").reshape(1024, 2 * width)

    back = lax.ppermute(product_block, ALL, [(b, a) for a, b in pairs])

    small = matmul(both_cols[:, width:], both_cols, (0, 0))
    cross, gram = small[:, :width], small[:, width:]
    row_ids = lax.broadcasted_iota(jnp.int32, (width, width), 0)
    col_ids = lax.broadcasted_iota(jnp.int32, (width, width), 1)
    packed = jnp.where(col_ids <= row_ids, gram, cross).reshape(16, 16, width)
    diagonal = jnp.sum(jnp.where(col_ids == row_ids, cross, 0.0), 1).reshape(16, 1, 16)
    diagonal = jnp.pad(diagonal, ((0, 0), (0, 0), (0, width - 16)))
    packed = jnp.concatenate([packed, diagonal], 1)
    packed, back = lax.optimization_barrier((packed, back))
    packed = exchange(packed, COLS).sum(0)

    gathered = lax.all_gather(jnp.concatenate([back, packed], 0), COLS, axis=0)
    product_rows = gathered[:, :BLOCK].reshape(512, width)
    packed = gathered[:, BLOCK : BLOCK + 16].reshape(width, width)
    diagonal = gathered[:, BLOCK + 16, :16].reshape(width, 1)
    flipped = packed.T
    gram = jnp.where(col_ids <= row_ids, packed, flipped)
    cross = jnp.where(col_ids > row_ids, packed, jnp.where(col_ids == row_ids, diagonal, flipped))

    factor = jnp.linalg.cholesky(gram)
    inverse = lax.linalg.triangular_solve(
        factor, jnp.eye(width, dtype=jnp.float32), left_side=True, lower=True
    )
    basis_rows = matmul(panel_rows, inverse, (1, 1))
    left = matmul(basis_rows, inverse, (1, 0))
    right = product_rows - matmul(left, cross, (1, 0))
    right = matmul(matmul(right, inverse, (1, 1)), inverse, (1, 0))
    updated = trailing - matmul(jnp.concatenate([left, right], 1), both_cols, (1, 1), high)
    return (updated, basis_rows)


def solution(mesh):
    fine = Mesh(mesh.devices.reshape(8, 4, 8, 2), ALL)
    return jax.shard_map(
        shards, mesh=fine, in_specs=(P(ROWS, COLS), P(ROWS, COLS)),
        out_specs=(P(ROWS, COLS), P(ROWS, None)), check_vma=False,
    )
```

time: 862 us -> 252 us (0.29)
  waiting for transfers between devices: 735 us -> 37.5 us
  starting transfers between devices: 0.21 us -> 48.9 us
  blocking collectives: 22.7 us -> 70.8 us
  between operations: 15.2 us -> 2.24 us
    psum x5 -> x0, waiting for transfers between devices: 735 us -> none  [the longest x2 314 us: spread(): return lax.psum(kept, axis)]
    all_to_all x0 -> x3, starting transfers between devices: none -> 36.6 us  [exchange(): return lax.all_to_all(value, axis, 0, 0, tiled=True)]
    all_to_all x0 -> x3, waiting for transfers between devices: none -> 35.1 us  [exchange(): return lax.all_to_all(value, axis, 0, 0, tiled=True)]
    all_to_all x0 -> x2, blocking collectives: none -> 30.9 us  [exchange(): return lax.all_to_all(value, axis, 0, 0, tiled=True)]
    all_gather x1 -> x2, blocking collectives: 22.7 us -> 39.9 us  [the longest x1 22.7 us: shards(): panel_rows = lax.all_gather(panel, COLS, axis=1, tiled=True)]
    ppermute x0 -> x2, starting transfers between devices: none -> 12.3 us  [the longest x1 10.4 us: shards(): back = lax.ppermute(product_block, ALL, [(b, a) for a, b in pairs])]
    another operation x10 -> x9, other arithmetic: 56 us -> 55.5 us  [the longest x6 34 us: shards(): factor = jnp.linalg.cholesky(gram)]
  transfers between devices with their start and end apart: 5 -> 5, of which waited for: 5 -> 4; matrix products, arithmetic and copies ran while one was open for 0% -> 3% of each run, Pallas kernels for 0% -> 0%
where the time goes in v1:
time: 252 us; the launch traced here: 251 us
  blocking collectives  70.8 us (28%)
  other arithmetic  58.2 us (23%)
  starting transfers between devices  48.9 us (19%)
  waiting for transfers between devices  37.5 us (15%)
  matrix products  19.5 us (8%)
  local copies, waits for them, and re-layouts  13.4 us (5%)
    all_to_all x3, starting transfers between devices, exchange(): return lax.all_to_all(value, axis, 0, 0, tiled=True)  36.6 us
    all_to_all x3, waiting for transfers between devices, exchange(): return lax.all_to_all(value, axis, 0, 0, tiled=True)  35.1 us
    another operation x6, other arithmetic, shards(): factor = jnp.linalg.cholesky(gram)  34 us
    all_to_all x2, blocking collectives, exchange(): return lax.all_to_all(value, axis, 0, 0, tiled=True)  30.9 us
    all_gather x1, blocking collectives, shards(): panel_rows = lax.all_gather(panel, COLS, axis=1, tiled=True)  22.7 us
    another operation x3, other arithmetic, shards(): lax.linalg.triangular_solve(factor, jnp.eye(width, dtype=jnp.float32), le...  21.5 us
    all_gather x1, blocking collectives, shards(): gathered = lax.all_gather(jnp.concatenate([back, packed], 0), COLS, axis=0)  17.2 us
    dot_general x8, matrix products, matmul(): lax.dot_general(left, right, ((contract[:1], contract[1:]), ((), ())), pr...  16.5 us
  transfers between devices with their start and end apart: 5, of which 4 were waited for; matrix products, arithmetic and copies ran while one was open for 3% of the time, Pallas kernels for 0%

profile of v1, /device:TPU:1, one launch (start us, length us, event | category | flops | bytes accessed | tf_op | source)
XLA Modules:
  0.0 250.8 jit_solution(10625310543495620284)
XLA Ops:
  0.6 22.7 %all_gather.9 = f32[512,256]{0,1:T(8,128)S(1)} all-gather(f32[512,16]{0,1:T(8,128)} %param.3), channel_id=1, replica_groups=mesh['z'=8,'x'=4,'y'=8,'c'=2] {'y','c'}, dimensions={1}, use_global_device_ids=true | all-gather | bytes 557056 | tf_op jit(solution)/shard_map/all_gather | solution.py:45
  23.4 2.0 collective-permute-start
  25.4 3.4 %fusion.24 = f32[1024,256]{1,0:T(8,128)S(1)} fusion(f32[512,1024]{1,0:T(8,128)} %param.2, f32[512,256]{0,1:T(8,128)S(1)} %all_gather.9), kind=kOutput, calls=%fused_computation.60 | convolution fusion | flops 805306368 | bytes 3670016 | tf_op jit(solution)/shard_map/dot_general | solution.py:13
  28.8 2.4 collective-permute-done
  31.2 15.4 %all_to_all.25 = f32[4,256,256]{2,1,0:T(8,128)S(1)} all-to-all(f32[4,256,256]{2,1,0:T(8,128)S(1)} %bitcast.59), channel_id=1, replica_groups=mesh['z'=8,'x'=4,'y'=8,'c'=2] {'x'}, dimensions={0} | all-to-all | bytes 2097152 | tf_op jit(solution)/shard_map/all_to_all | solution.py:20
  46.6 0.8 reduce_sum.36
  47.4 20.3 %all-to-all-start.1 = ((f32[8,32,256]{2,1,0:T(8,128)}), f32[8,32,256]{2,1,0:T(8,128)S(1)}, u32[]{:S(2)}, u32[]{:S(2)}) async-start(f32[8,32,256]{2,1,0:T(8,128)} %bitcast.1), calls=%async_computation.1 | async-start | bytes 524288 | tf_op jit(solution)/shard_map/all_to_all | solution.py:20
  67.8 9.3 %all-to-all-done.1 = f32[8,32,256]{2,1,0:T(8,128)S(1)} async-done(((f32[8,32,256]{2,1,0:T(8,128)}), f32[8,32,256]{2,1,0:T(8,128)S(1)}, u32[]{:S(2)}, u32[]{:S(2)}) %all-to-all-start.1) | async-done | bytes 262176 | tf_op jit(solution)/shard_map/all_to_all | solution.py:20
  77.2 15.5 %all_to_all.26 = f32[8,32,512]{2,1,0:T(8,128)S(1)} all-to-all(f32[8,32,512]{2,1,0:T(8,128)S(1)} %broadcast_in_dim.29), channel_id=1, replica_groups=mesh['z'=8,'x'=4,'y'=8,'c'=2] {'z'}, dimensions={0} | all-to-all | bytes 1048576 | tf_op jit(solution)/shard_map/all_to_all | solution.py:20
  92.7 1.6 broadcast_in_dim.31
  94.3 3.6 %all-to-all-start.3 = ((f32[4,256,512]{2,1,0:T(8,128)}), f32[4,256,512]{2,1,0:T(8,128)S(1)}, u32[]{:S(2)}, u32[]{:S(2)}) async-start(f32[4,256,512]{2,1,0:T(8,128)} %broadcast_in_dim.31), calls=%async_computation.3 | async-start | bytes 4194304 | tf_op jit(solution)/shard_map/all_to_all | solution.py:20
  97.9 10.4 %collective-permute-start.1 = (f32[32,256]{1,0:T(8,128)S(1)}, f32[32,256]{1,0:T(8,128)S(1)}, u32[]{:S(2)}, u32[]{:S(2)}) collective-permute-start(f32[32,256]{1,0:T(8,128)S(1)} %reduce_sum.37), channel_id=1, source_target_pairs={{0,0},{1,32},{2,64},{3,96},{4,128},{5,160},{6,192},{7,224},{8,256}... | collective-permute-start | bytes 98312 | tf_op jit(solution)/shard_map/ppermute | solution.py:58
  108.3 11.3 %all-to-all-done.3 = f32[4,256,512]{2,1,0:T(8,128)S(1)} async-done(((f32[4,256,512]{2,1,0:T(8,128)}), f32[4,256,512]{2,1,0:T(8,128)S(1)}, u32[]{:S(2)}, u32[]{:S(2)}) %all-to-all-start.3) | async-done | bytes 2097184 | tf_op jit(solution)/shard_map/all_to_all | solution.py:20
  119.5 3.4 %fusion = f32[256,512]{0,1:T(8,128)S(1)} fusion(f32[1024,512]{1,0:T(8,128)S(1)} %bitcast.56), kind=kOutput, calls=%fused_computation.6 | convolution fusion | flops 1610612736 | bytes 3670016 | tf_op jit(solution)/shard_map/dot_general | solution.py:13
  123.3 0.8 select_maximum_fusion
  124.0 12.7 %all-to-all-start.4 = ((f32[16,17,256]{2,1,0:T(8,128)}), f32[16,17,256]{2,1,0:T(8,128)S(1)}, u32[]{:S(2)}, u32[]{:S(2)}) async-start(f32[16,17,256]{2,1,0:T(8,128)} %select_maximum_fusion), calls=%async_computation.4 | async-start | bytes 786432 | tf_op jit(solution)/shard_map/all_to_all | solution.py:20
  136.8 14.5 %all-to-all-done.4 = f32[16,17,256]{2,1,0:T(8,128)S(1)} async-done(((f32[16,17,256]{2,1,0:T(8,128)}), f32[16,17,256]{2,1,0:T(8,128)S(1)}, u32[]{:S(2)}, u32[]{:S(2)}) %all-to-all-start.4) | async-done | bytes 278560 | tf_op jit(solution)/shard_map/all_to_all | solution.py:20
  151.3 17.2 %all-gather.1 = f32[16,49,256]{2,1,0:T(8,128)S(1)} all-gather(f32[1,49,256]{2,1,0:T(8,128)S(1)} %maximum_bitcast_fusion), channel_id=2, replica_groups=mesh['z'=8,'x'=4,'y'=8,'c'=2] {'y','c'}, dimensions={0}, use_global_device_ids=true | all-gather | bytes 852992 | tf_op jit(solution)/shard_map/all_gather | solution.py:71
  168.6 0.8 slice.82
  169.5 0.8 copy.60
  170.3 1.0 fusion.5
  171.5 0.7 copy-done.1
  172.2 11.7 %cholesky.49 = f32[128,128]{1,0:T(8,128)S(1)} custom-call(f32[128,128]{1,0:T(8,128)S(1)} %cholesky.115), custom_call_target="Cholesky" | custom-call | tf_op jit(solution)/shard_map/jit(cholesky)/cholesky | solution.py:79
  184.1 9.8 %custom-call.14 = f32[1,128,128]{1,2,0:T(8,128)S(1)} custom-call(f32[1,128,128]{2,1,0:T(8,128)S(1)} %get-tuple-element.61), custom_call_target="InvertDiagBlocksLowerTriangular" | custom-call | tf_op jit(solution)/shard_map/jit(cholesky)/cholesky | solution.py:79
  193.9 1.0 fusion.15
  194.9 1.1 convolution_subtract_fusion.3
  196.1 11.7 %cholesky.103 = f32[128,128]{1,0:T(8,128)S(1)} custom-call(f32[128,128]{1,0:T(8,128)S(1)} %convolution_subtract_fusion.3), custom_call_target="Cholesky" | custom-call | tf_op jit(solution)/shard_map/jit(cholesky)/cholesky | solution.py:79
  208.0 0.7 cholesky.111
  208.7 0.7 compare_reduce_fusion
  210.7 0.6 constant_dynamic-update-slice_fusion.1
  211.4 0.6 constant_dynamic-update-slice_fusion
  212.0 1.0 select_select_fusion
  213.1 5.7 %while.1 = (s32[]{:T(128)}, f32[256,256]{0,1:T(8,128)S(1)}, s32[2,2]{1,0:T(2,128)S(1)}, f32[2,128,128]{2,1,0:T(8,128)}, s32[]{:T(128)}) while((s32[]{:T(128)}, f32[256,256]{0,1:T(8,128)S(1)}, s32[2,2]{1,0:T(2,128)S(1)}, f32[2,128,128]{2,1,0:T(8,128)}, s32[]{:T(128)}) %tuple.41), condition=%wide.while_cond, body=%wide.while_body.sunk | while | flops 2 | bytes 393329 | solution.py:80
  213.2 0.6 fusion.40
  213.8 1.4 dynamic-slice.7
  215.4 0.6 bitcast_dynamic-update-slice_fusion.2
  216.0 0.6 fusion.40
  216.6 1.4 dynamic-slice.7
  218.1 0.6 bitcast_dynamic-update-slice_fusion.2
  218.7 20.5 %custom-call.15 = f32[2,128,128]{1,2,0:T(8,128)S(1)} custom-call(f32[2,128,128]{2,1,0:T(8,128)} %get-tuple-element.15), custom_call_target="InvertDiagBlocksLowerTriangular" | custom-call | tf_op jit(solution)/shard_map/triangular_solve | solution.py:80
  239.5 0.3 convolution_subtract_fusion.2
  240.1 0.6 fusion.12
  240.8 0.7 fusion.11
  241.5 2.2 convolution_subtract_fusion.1
  243.6 0.6 fusion.10
  244.3 0.7 fusion.9
  245.0 4.9 %convolution_subtract_fusion = f32[512,1024]{1,0:T(8,128)} fusion(f32[512,1024]{1,0:T(8,128)S(1)} %copy-done, f32[1024,512]{1,0:T(8,128)S(1)} %bitcast.57, f32[512,256]{0,1:T(8,128)S(1)} %fusion.9, f32[512,256]{0,1:T(8,128)S(1)} %fusion.11), kind=kOutput, calls=%fused_computation.2 | convolution fusion | flops 1611399168 | bytes 7340032 | tf_op jit(solution)/shard_map/dot_general | solution.py:13
  249.8 1.0 copy.67
  (35 shorter events, 2.1 us)
Async XLA Ops:
  23.4 7.8 %collective-permute-start = (f32[32,256]{0,1:T(8,128)S(1)}, f32[32,256]{0,1:T(8,128)S(1)}, u32[]{:S(2)}, u32[]{:S(2)}) collective-permute-start(f32[32,256]{0,1:T(8,128)S(1)} %constant_dynamic-slice_fusion.1), channel_id=1, source_target_pairs={{0,0},{32,1},{64,2},{96,3},{128,4},{160,5},{192,6},{224,7},{256,8}... | collective-permute-start | bytes 98312 | tf_op jit(solution)/shard_map/ppermute | solution.py:47
  47.4 29.7 %all-to-all-start.1 = ((f32[8,32,256]{2,1,0:T(8,128)}), f32[8,32,256]{2,1,0:T(8,128)S(1)}, u32[]{:S(2)}, u32[]{:S(2)}) async-start(f32[8,32,256]{2,1,0:T(8,128)} %bitcast.1), calls=%async_computation.1 | async-start | bytes 524288 | tf_op jit(solution)/shard_map/all_to_all | solution.py:20
  94.3 25.3 %all-to-all-start.3 = ((f32[4,256,512]{2,1,0:T(8,128)}), f32[4,256,512]{2,1,0:T(8,128)S(1)}, u32[]{:S(2)}, u32[]{:S(2)}) async-start(f32[4,256,512]{2,1,0:T(8,128)} %broadcast_in_dim.31), calls=%async_computation.3 | async-start | bytes 4194304 | tf_op jit(solution)/shard_map/all_to_all | solution.py:20
  97.9 26.2 %collective-permute-start.1 = (f32[32,256]{1,0:T(8,128)S(1)}, f32[32,256]{1,0:T(8,128)S(1)}, u32[]{:S(2)}, u32[]{:S(2)}) collective-permute-start(f32[32,256]{1,0:T(8,128)S(1)} %reduce_sum.37), channel_id=1, source_target_pairs={{0,0},{1,32},{2,64},{3,96},{4,128},{5,160},{6,192},{7,224},{8,256}... | collective-permute-start | bytes 98312 | tf_op jit(solution)/shard_map/ppermute | solution.py:58
  124.0 27.2 %all-to-all-start.4 = ((f32[16,17,256]{2,1,0:T(8,128)}), f32[16,17,256]{2,1,0:T(8,128)S(1)}, u32[]{:S(2)}, u32[]{:S(2)}) async-start(f32[16,17,256]{2,1,0:T(8,128)} %select_maximum_fusion), calls=%async_computation.4 | async-start | bytes 786432 | tf_op jit(solution)/shard_map/all_to_all | solution.py:20
  171.5 0.7 copy-start.1
  241.4 3.5 %copy-start = (f32[512,1024]{1,0:T(8,128)S(1)}, f32[512,1024]{1,0:T(8,128)}, u32[]{:S(2)}) copy-start(f32[512,1024]{1,0:T(8,128)} %param.2) | copy-start | bytes 6291460

commit v2 on v1

v2 whole, which is shorter than its diff:
```python
import jax
import jax.numpy as jnp
from jax import lax
from jax.experimental import pallas as pl
from jax.experimental.pallas import tpu as pltpu
from jax.sharding import Mesh, PartitionSpec as P

ROWS = ("z", "x")
COLS = ("y", "c")
ALL = ("z", "x", "y", "c")
BLOCK = 32


def matmul(left, right, contract, precision=lax.Precision.HIGHEST):
    return lax.dot_general(
        left, right, ((contract[:1], contract[1:]), ((), ())),
        precision=precision, preferred_element_type=jnp.float32,
    )


def iota(shape, dimension):
    return lax.broadcasted_iota(jnp.int32, shape, dimension)


def whole(value):
    return jnp.broadcast_to(value, (8, 128))


def inverse_of_block(tile, offset, size):
    start = 0 if offset else size
    lane, row = iota((size, 128), 1), iota((size, 128), 0)
    inside = (lane >= offset) & (lane < offset + size)
    work = jnp.where(inside, tile, jnp.where(lane == row + start, 1.0, 0.0))
    count = size // 8
    parts = [work[8 * i : 8 * i + 8] for i in range(count)]
    sub = iota((8, 128), 0)
    done = []
    for q in range(count):
        first = offset + 8 * q
        cols = [
            [whole(part[:, first + j : first + j + 1]) for j in range(8)]
            for part in parts[q:]
        ]
        pivots = {(i, j): whole(cols[0][j][i : i + 1]) for j in range(8) for i in range(j, 8)}
        rows = [whole(parts[q][i : i + 1]) for i in range(8)]
        inverses = []
        for j in range(8):
            inverses.append(1.0 / pivots[j, j])
            factors = {i: pivots[i, j] * inverses[j] for i in range(j + 1, 8)}
            for m in range(j + 1, 8):
                for i in range(m, 8):
                    pivots[i, m] = pivots[i, m] - factors[i] * pivots[m, j]
            for i in range(j + 1, 8):
                rows[i] = rows[i] - factors[i] * rows[j]
                for part in cols[1:]:
                    part[i] = part[i] - factors[i] * part[j]
        scaled = [row_j * inverse for row_j, inverse in zip(rows, inverses)]
        for i in range(q + 1, count):
            total = cols[i - q][0] * scaled[0]
            for j in range(1, 8):
                total = total + cols[i - q][j] * scaled[j]
            parts[i] = parts[i] - total
        final = rows[0] / jnp.sqrt(pivots[0, 0])
        for j in range(1, 8):
            final = jnp.where(sub == j, rows[j] / jnp.sqrt(pivots[j, j]), final)
        done.append(final)
    return jnp.concatenate(done, 0)[:, start : start + size]


def finish_kernel(gathered_ref, panel_ref, basis_ref, left_ref, work_ref, inverse_ref):
    width = panel_ref.shape[0]
    panel = panel_ref[...]
    packed = jnp.concatenate([gathered_ref[j, BLOCK : BLOCK + 16] for j in range(16)], 0)
    diagonal = gathered_ref[0, BLOCK + 16 : BLOCK + 17]
    for j in range(1, 16):
        diagonal = diagonal + gathered_ref[j, BLOCK + 16 : BLOCK + 17]
    row, col = iota((width, width), 0), iota((width, width), 1)
    flipped = packed.T
    work_ref[:, :width] = jnp.where(col <= row, packed, flipped)
    work_ref[:, width:] = jnp.where(col == row, 1.0, 0.0)
    size = 64
    for k in range(0, width, size):
        tile = k // 128 * 128
        block = inverse_of_block(work_ref[k : k + size, tile : tile + 128], k - tile, size)
        rows = matmul(block, work_ref[k : k + size, :], (1, 0))
        inverse_ref[k : k + size, :] = rows[:, width:]
        if k + size < width:
            below = matmul(rows[:, k + size : width], rows, (0, 0))
            work_ref[k + size :, :] = work_ref[k + size :, :] - below
    cross = jnp.where(col > row, packed, jnp.where(col == row, diagonal, flipped))
    inverse = inverse_ref[...]
    whole_inverse = matmul(inverse, inverse, (0, 0))
    product = jnp.concatenate([gathered_ref[j, :BLOCK] for j in range(16)], 0)
    basis_ref[...] = matmul(panel, inverse, (0, 1))
    left = matmul(panel, whole_inverse, (0, 0))
    left_ref[:, :width] = left
    left_ref[:, width:] = matmul(product - matmul(left, cross, (1, 0)), whole_inverse, (1, 0))


def finish(gathered, panel):
    width, rows = panel.shape
    return pl.pallas_call(
        finish_kernel,
        out_shape=(
            jax.ShapeDtypeStruct((rows, width), jnp.float32),
            jax.ShapeDtypeStruct((rows, 2 * width), jnp.float32),
        ),
        scratch_shapes=[
            pltpu.VMEM((width, 2 * width), jnp.float32),
            pltpu.VMEM((width, width), jnp.float32),
        ],
        compiler_params=pltpu.CompilerParams(vmem_limit_bytes=32 * 2**20),
        cost_estimate=pl.CostEstimate(flops=2 * 10**9, bytes_accessed=4 * 10**6, transcendentals=0),
        name="finish",
    )(gathered, panel)


def exchange(value, axis):
    return lax.all_to_all(value, axis, 0, 0, tiled=True)


def repeat(value, count):
    return jnp.broadcast_to(value[None], (count, *value.shape))


def blocks_of_columns():
    pairs = []
    for z in range(8):
        for x in range(4):
            for col in range(16):
                part = 8 * x + z
                row = 2 * col + part // 16
                pairs.append((row * 16 + part % 16, (z * 4 + x) * 16 + col))
    return pairs


def shards(trailing, panel):
    width = panel.shape[1] * lax.axis_size(COLS)
    column = lax.axis_index(COLS)
    pairs = blocks_of_columns()
    high = lax.Precision.HIGH

    panel_rows = lax.all_gather(panel, COLS, axis=1, tiled=True)
    block = lax.dynamic_slice(panel_rows, (column * BLOCK, 0), (BLOCK, width))
    panel_block = lax.ppermute(block, ALL, pairs)

    partial = matmul(trailing, panel_rows, (0, 0), high)
    partial = lax.optimization_barrier((partial, panel_block))[0]
    partial = exchange(partial.reshape(4, 256, width), "x").sum(0)
    product_block = exchange(partial.reshape(8, BLOCK, width), "z").sum(0)

    both = jnp.concatenate([product_block, panel_block], 1)
    both = exchange(repeat(both, 8), "z").reshape(256, 2 * width)
    both_cols = exchange(repeat(both, 4), "x").reshape(1024, 2 * width)

    back = lax.ppermute(product_block, ALL, [(b, a) for a, b in pairs])

    small = matmul(both_cols[:, width:], both_cols, (0, 0))
    cross, gram = small[:, :width], small[:, width:]
    row, col = iota((width, width), 0), iota((width, width), 1)
    packed = jnp.where(col <= row, gram, cross).reshape(16, 16, width)
    diagonal = jnp.sum(jnp.where(col == row, cross, 0.0), 0)
    own = iota((16, 1, width), 0) == iota((16, 1, width), 2) // 16
    packed = jnp.concatenate([packed, jnp.where(own, diagonal, 0.0)], 1)
    packed, back = lax.optimization_barrier((packed, back))
    packed = exchange(packed, COLS).sum(0)

    gathered = lax.all_gather(jnp.concatenate([back, packed], 0), COLS, axis=0)
    basis_rows, left = finish(gathered, panel_rows.T)
    updated = trailing - matmul(left, both_cols, (1, 1), high)
    return (updated, basis_rows)


def solution(mesh):
    fine = Mesh(mesh.devices.reshape(8, 4, 8, 2), ALL)
    return jax.shard_map(
        shards, mesh=fine, in_specs=(P(ROWS, COLS), P(ROWS, COLS)),
        out_specs=(P(ROWS, COLS), P(ROWS, None)), check_vma=False,
    )
```

time: 252 us -> 183 us (0.73)
  other arithmetic: 58.2 us -> 0.96 us
  blocking collectives: 70.8 us -> 97.8 us
  waiting for transfers between devices: 37.5 us -> 23 us
  Pallas kernels: 0 us -> 13 us
  starting transfers between devices: 48.9 us -> 36.2 us
  local copies, waits for them, and re-layouts: 13.4 us -> 1.8 us
  matrix products: 19.5 us -> 8.51 us
    another operation x9 -> x0, other arithmetic: 55.5 us -> none  [the longest x6 34 us: shards(): factor = jnp.linalg.cholesky(gram)]
    all_to_all x2 -> x3, blocking collectives: 30.9 us -> 57.9 us  [exchange(): return lax.all_to_all(value, axis, 0, 0, tiled=True)]
    all_to_all x3 -> x2, waiting for transfers between devices: 35.1 us -> 20.6 us  [exchange(): return lax.all_to_all(value, axis, 0, 0, tiled=True)]
    pallas_call x0 -> x1, Pallas kernels: none -> 13 us  [finish(): pl.pallas_call(finish_kernel, out_shape=(jax.ShapeDtypeStruct((rows, widt...]
    all_to_all x3 -> x2, starting transfers between devices: 36.6 us -> 23.9 us  [exchange(): return lax.all_to_all(value, axis, 0, 0, tiled=True)]
    dot_general x8 -> x3, matrix products: 16.5 us -> 8.51 us  [matmul(): lax.dot_general(left, right, ((contract[:1], contract[1:]), ((), ())), pr...]
    another operation x18 -> x0, local copies, waits for them, and re-layouts: 7.8 us -> none
    another operation x5 -> x0, matrix products: 3.04 us -> none  [the longest x2 2.15 us: shards(): factor = jnp.linalg.cholesky(gram)]
  transfers between devices with their start and end apart: 5 -> 4, of which waited for: 4 -> 3; matrix products, arithmetic and copies ran while one was open for 3% -> 3% of each run, Pallas kernels for 0% -> 0%
where the time goes in v2:
time: 183 us; the launch traced here: 182 us
  blocking collectives  97.8 us (53%)
  starting transfers between devices  36.2 us (20%)
  waiting for transfers between devices  23 us (13%)
  Pallas kernels  13 us (7%)
  matrix products  8.51 us (5%)
    all_to_all x3, blocking collectives, exchange(): return lax.all_to_all(value, axis, 0, 0, tiled=True)  57.9 us
    all_to_all x2, starting transfers between devices, exchange(): return lax.all_to_all(value, axis, 0, 0, tiled=True)  23.9 us
    all_gather x1, blocking collectives, shards(): panel_rows = lax.all_gather(panel, COLS, axis=1, tiled=True)  22.7 us
    all_to_all x2, waiting for transfers between devices, exchange(): return lax.all_to_all(value, axis, 0, 0, tiled=True)  20.6 us
    all_gather x1, blocking collectives, shards(): gathered = lax.all_gather(jnp.concatenate([back, packed], 0), COLS, axis=0)  17.2 us
    pallas_call x1, Pallas kernels, finish(): pl.pallas_call(finish_kernel, out_shape=(jax.ShapeDtypeStruct((rows, widt...  13 us
    ppermute x1, starting transfers between devices, shards(): back = lax.ppermute(product_block, ALL, [(b, a) for a, b in pairs])  10.4 us
    dot_general x3, matrix products, matmul(): lax.dot_general(left, right, ((contract[:1], contract[1:]), ((), ())), pr...  8.51 us
  transfers between devices with their start and end apart: 4, of which 3 were waited for; matrix products, arithmetic and copies ran while one was open for 3% of the time, Pallas kernels for 0%

profile of v2, /device:TPU:1, one launch (start us, length us, event | category | flops | bytes accessed | tf_op | source)
XLA Modules:
  0.0 182.0 jit_solution(9025920117426944288)
XLA Ops:
  0.6 22.7 %all_gather.9 = f32[512,256]{0,1:T(8,128)S(1)} all-gather(f32[512,16]{0,1:T(8,128)} %param.3), channel_id=1, replica_groups=mesh['z'=8,'x'=4,'y'=8,'c'=2] {'y','c'}, dimensions={1}, use_global_device_ids=true | all-gather | bytes 557056 | tf_op jit(solution)/shard_map/all_gather | solution.py:143
  23.3 0.1 constant_dynamic-slice_fusion
  23.4 2.0 %collective-permute-start = (f32[32,256]{0,1:T(8,128)S(1)}, f32[32,256]{0,1:T(8,128)S(1)}, u32[]{:S(2)}, u32[]{:S(2)}) collective-permute-start(f32[32,256]{0,1:T(8,128)S(1)} %constant_dynamic-slice_fusion), channel_id=1, source_target_pairs={{0,0},{32,1},{64,2},{96,3},{128,4},{160,5},{192,6},{224,7},{256,8}... | collective-permute-start | bytes 98312 | tf_op jit(solution)/shard_map/ppermute | solution.py:145
  25.4 3.4 %fusion.2 = f32[1024,256]{1,0:T(8,128)S(1)} fusion(f32[512,1024]{1,0:T(8,128)} %param.2, f32[512,256]{0,1:T(8,128)S(1)} %all_gather.9), kind=kOutput, calls=%fused_computation.18 | convolution fusion | flops 805306368 | bytes 3670016 | tf_op jit(solution)/shard_map/dot_general | solution.py:15
  28.8 2.4 %collective-permute-done = f32[32,256]{0,1:T(8,128)S(1)} collective-permute-done((f32[32,256]{0,1:T(8,128)S(1)}, f32[32,256]{0,1:T(8,128)S(1)}, u32[]{:S(2)}, u32[]{:S(2)}) %collective-permute-start) | collective-permute-done | bytes 32800 | tf_op jit(solution)/shard_map/ppermute | solution.py:145
  31.2 15.4 %all_to_all.25 = f32[4,256,256]{2,1,0:T(8,128)S(1)} all-to-all(f32[4,256,256]{2,1,0:T(8,128)S(1)} %bitcast.16), channel_id=1, replica_groups=mesh['z'=8,'x'=4,'y'=8,'c'=2] {'x'}, dimensions={0} | all-to-all | bytes 2097152 | tf_op jit(solution)/shard_map/all_to_all | solution.py:119
  46.6 0.8 reduce_sum.36
  47.4 20.3 %all-to-all-start.1 = ((f32[8,32,256]{2,1,0:T(8,128)}), f32[8,32,256]{2,1,0:T(8,128)S(1)}, u32[]{:S(2)}, u32[]{:S(2)}) async-start(f32[8,32,256]{2,1,0:T(8,128)} %bitcast.1), calls=%async_computation.1 | async-start | bytes 524288 | tf_op jit(solution)/shard_map/all_to_all | solution.py:119
  67.7 0.1 copy.7
  67.8 9.3 %all-to-all-done.1 = f32[8,32,256]{2,1,0:T(8,128)S(1)} async-done(((f32[8,32,256]{2,1,0:T(8,128)}), f32[8,32,256]{2,1,0:T(8,128)S(1)}, u32[]{:S(2)}, u32[]{:S(2)}) %all-to-all-start.1) | async-done | bytes 262176 | tf_op jit(solution)/shard_map/all_to_all | solution.py:119
  77.1 0.1 broadcast_in_dim.25
  77.2 15.5 %all_to_all.26 = f32[8,32,512]{2,1,0:T(8,128)S(1)} all-to-all(f32[8,32,512]{2,1,0:T(8,128)S(1)} %broadcast_in_dim.25), channel_id=1, replica_groups=mesh['z'=8,'x'=4,'y'=8,'c'=2] {'z'}, dimensions={0} | all-to-all | bytes 1048576 | tf_op jit(solution)/shard_map/all_to_all | solution.py:119
  92.7 1.6 broadcast_in_dim.27
  94.3 3.6 %all-to-all-start.3 = ((f32[4,256,512]{2,1,0:T(8,128)}), f32[4,256,512]{2,1,0:T(8,128)S(1)}, u32[]{:S(2)}, u32[]{:S(2)}) async-start(f32[4,256,512]{2,1,0:T(8,128)} %broadcast_in_dim.27), calls=%async_computation.3 | async-start | bytes 4194304 | tf_op jit(solution)/shard_map/all_to_all | solution.py:119
  97.9 10.4 %collective-permute-start.1 = (f32[32,256]{1,0:T(8,128)S(1)}, f32[32,256]{1,0:T(8,128)S(1)}, u32[]{:S(2)}, u32[]{:S(2)}) collective-permute-start(f32[32,256]{1,0:T(8,128)S(1)} %reduce_sum.37), channel_id=1, source_target_pairs={{0,0},{1,32},{2,64},{3,96},{4,128},{5,160},{6,192},{7,224},{8,256}... | collective-permute-start | bytes 98312 | tf_op jit(solution)/shard_map/ppermute | solution.py:156
  108.3 11.3 %all-to-all-done.3 = f32[4,256,512]{2,1,0:T(8,128)S(1)} async-done(((f32[4,256,512]{2,1,0:T(8,128)}), f32[4,256,512]{2,1,0:T(8,128)S(1)}, u32[]{:S(2)}, u32[]{:S(2)}) %all-to-all-start.3) | async-done | bytes 2097184 | tf_op jit(solution)/shard_map/all_to_all | solution.py:119
  119.5 1.9 %fusion = f32[256,512]{1,0:T(8,128)S(1)} fusion(f32[1024,512]{1,0:T(8,128)S(1)} %bitcast.14), kind=kOutput, calls=%fused_computation.1 | convolution fusion | flops 1610612736 | bytes 3670016 | tf_op jit(solution)/shard_map/dot_general | solution.py:15
  121.5 0.1 slice_select_fusion
  121.6 0.0 collective-permute-done.1
  121.6 27.0 %all_to_all.27 = f32[16,17,256]{2,1,0:T(8,128)S(1)} all-to-all(f32[16,17,256]{2,1,0:T(8,128)S(1)} %pad_maximum_fusion), channel_id=1, replica_groups=mesh['z'=8,'x'=4,'y'=8,'c'=2] {'y','c'}, dimensions={0} | all-to-all | bytes 557056 | tf_op jit(solution)/shard_map/all_to_all | solution.py:119
  148.7 17.2 %all-gather.1.gathered_ref = f32[16,49,256]{2,1,0:T(8,128)S(1)} all-gather(f32[1,49,256]{2,1,0:T(8,128)S(1)} %maximum_bitcast_fusion), channel_id=2, replica_groups=mesh['z'=8,'x'=4,'y'=8,'c'=2] {'y','c'}, dimensions={0}, use_global_device_ids=true | all-gather | bytes 852992 | tf_op jit(solution)/shard_map/all_gather | solution.py:168
  165.9 0.0 copy-start
  165.9 13.0 %finish.1 = (f32[512,256]{1,0:T(8,128)}, f32[512,512]{1,0:T(8,128)S(1)}) custom-call(f32[16,49,256]{2,1,0:T(8,128)S(1)} %all-gather.1.gathered_ref, f32[256,512]{1,0:T(8,128)S(1)} %bitcast.13), custom_call_target="tpu_custom_call" | custom-call | flops 2000000000 | bytes 4000000 | tf_op jit(solution)/shard_map/finish/pallas_call | solution.py:102
  178.8 0.0 copy-done
  178.9 3.2 %convolution_subtract_fusion = f32[512,1024]{1,0:T(8,128)} fusion(f32[512,1024]{1,0:T(8,128)S(1)} %copy-done, f32[512,512]{1,0:T(8,128)S(1)} %get-tuple-element.10, f32[1024,512]{1,0:T(8,128)S(1)} %bitcast.15), kind=kOutput, calls=%fused_computation | convolution fusion | flops 1611137024 | bytes 7340032 | tf_op jit(solution)/shard_map/dot_general | solution.py:15
  (8 shorter events, 0.1 us)
Async XLA Ops:
  23.4 7.8 %collective-permute-start = (f32[32,256]{0,1:T(8,128)S(1)}, f32[32,256]{0,1:T(8,128)S(1)}, u32[]{:S(2)}, u32[]{:S(2)}) collective-permute-start(f32[32,256]{0,1:T(8,128)S(1)} %constant_dynamic-slice_fusion), channel_id=1, source_target_pairs={{0,0},{32,1},{64,2},{96,3},{128,4},{160,5},{192,6},{224,7},{256,8}... | collective-permute-start | bytes 98312 | tf_op jit(solution)/shard_map/ppermute | solution.py:145
  47.4 29.7 %all-to-all-start.1 = ((f32[8,32,256]{2,1,0:T(8,128)}), f32[8,32,256]{2,1,0:T(8,128)S(1)}, u32[]{:S(2)}, u32[]{:S(2)}) async-start(f32[8,32,256]{2,1,0:T(8,128)} %bitcast.1), calls=%async_computation.1 | async-start | bytes 524288 | tf_op jit(solution)/shard_map/all_to_all | solution.py:119
  94.3 25.3 %all-to-all-start.3 = ((f32[4,256,512]{2,1,0:T(8,128)}), f32[4,256,512]{2,1,0:T(8,128)S(1)}, u32[]{:S(2)}, u32[]{:S(2)}) async-start(f32[4,256,512]{2,1,0:T(8,128)} %broadcast_in_dim.27), calls=%async_computation.3 | async-start | bytes 4194304 | tf_op jit(solution)/shard_map/all_to_all | solution.py:119
  97.9 23.7 %collective-permute-start.1 = (f32[32,256]{1,0:T(8,128)S(1)}, f32[32,256]{1,0:T(8,128)S(1)}, u32[]{:S(2)}, u32[]{:S(2)}) collective-permute-start(f32[32,256]{1,0:T(8,128)S(1)} %reduce_sum.37), channel_id=1, source_target_pairs={{0,0},{1,32},{2,64},{3,96},{4,128},{5,160},{6,192},{7,224},{8,256}... | collective-permute-start | bytes 98312 | tf_op jit(solution)/shard_map/ppermute | solution.py:156
  165.9 13.0 %copy-start = (f32[512,1024]{1,0:T(8,128)S(1)}, f32[512,1024]{1,0:T(8,128)}, u32[]{:S(2)}) copy-start(f32[512,1024]{1,0:T(8,128)} %param.2) | copy-start | bytes 6291460

commit v3 on v2

--- a/solution.py
+++ b/solution.py
@@ -49,7 +49,7 @@
             factors = {i: pivots[i, j] * inverses[j] for i in range(j + 1, 8)}
             for m in range(j + 1, 8):
                 for i in range(m, 8):
-                    pivots[i, m] = pivots[i, m] - factors[i] * pivots[m, j]
+                    pivots[i, m] = pivots[i, m] - pivots[i, j] * pivots[m, j] * inverses[j]
             for i in range(j + 1, 8):
                 rows[i] = rows[i] - factors[i] * rows[j]
                 for part in cols[1:]:
@@ -90,7 +90,7 @@
     cross = jnp.where(col > row, packed, jnp.where(col == row, diagonal, flipped))
     inverse = inverse_ref[...]
     whole_inverse = matmul(inverse, inverse, (0, 0))
-    product = jnp.concatenate([gathered_ref[j, :BLOCK] for j in range(16)], 0)
+    product = jnp.concatenate([gathered_ref[2 * (j % 8) + j // 8, :BLOCK] for j in range(16)], 0)
     basis_ref[...] = matmul(panel, inverse, (0, 1))
     left = matmul(panel, whole_inverse, (0, 0))
     left_ref[:, :width] = left
@@ -128,25 +128,26 @@
     for z in range(8):
         for x in range(4):
             for col in range(16):
-                part = 8 * x + z
-                row = 2 * col + part // 16
-                pairs.append((row * 16 + part % 16, (z * 4 + x) * 16 + col))
+                row = 2 * col + x // 2
+                source = 2 * z + x % 2
+                pairs.append((row * 16 + source, (z * 4 + x) * 16 + col))
     return pairs
 
 
 def shards(trailing, panel):
     width = panel.shape[1] * lax.axis_size(COLS)
-    column = lax.axis_index(COLS)
+    place = 8 * lax.axis_index("c") + lax.axis_index("y")
     pairs = blocks_of_columns()
     high = lax.Precision.HIGH
 
     panel_rows = lax.all_gather(panel, COLS, axis=1, tiled=True)
-    block = lax.dynamic_slice(panel_rows, (column * BLOCK, 0), (BLOCK, width))
+    block = lax.dynamic_slice(panel_rows, (place * BLOCK, 0), (BLOCK, width))
     panel_block = lax.ppermute(block, ALL, pairs)
 
     partial = matmul(trailing, panel_rows, (0, 0), high)
-    partial = lax.optimization_barrier((partial, panel_block))[0]
-    partial = exchange(partial.reshape(4, 256, width), "x").sum(0)
+    partial = exchange(partial.reshape(4, 256, width), "x")
+    partial, panel_block = lax.optimization_barrier((partial, panel_block))
+    partial = partial.sum(0)
     product_block = exchange(partial.reshape(8, BLOCK, width), "z").sum(0)
 
     both = jnp.concatenate([product_block, panel_block], 1)
@@ -162,8 +163,10 @@
     diagonal = jnp.sum(jnp.where(col == row, cross, 0.0), 0)
     own = iota((16, 1, width), 0) == iota((16, 1, width), 2) // 16
     packed = jnp.concatenate([packed, jnp.where(own, diagonal, 0.0)], 1)
+    packed = packed.reshape(8, 2, 17, width).transpose(1, 0, 2, 3)
     packed, back = lax.optimization_barrier((packed, back))
-    packed = exchange(packed, COLS).sum(0)
+    packed = exchange(packed, "c").sum(0)
+    packed = exchange(packed, "y").sum(0)
 
     gathered = lax.all_gather(jnp.concatenate([back, packed], 0), COLS, axis=0)
     basis_rows, left = finish(gathered, panel_rows.T)

time: 183 us -> 180 us (0.984)
  waiting for transfers between devices: 23 us -> 44.4 us
  blocking collectives: 97.8 us -> 79.4 us
  starting transfers between devices: 36.2 us -> 29.5 us
    all_to_all x3, blocking collectives: 57.9 us -> 37.5 us  [exchange(): return lax.all_to_all(value, axis, 0, 0, tiled=True)]
    all_to_all x2 -> x3, waiting for transfers between devices: 20.6 us -> 31.4 us  [exchange(): return lax.all_to_all(value, axis, 0, 0, tiled=True)]
    ppermute x1, waiting for transfers between devices: 2.41 us -> 13 us  [shards(): panel_block = lax.ppermute(block, ALL, pairs)]
    ppermute x1, starting transfers between devices: 10.4 us -> 5.39 us  [shards(): back = lax.ppermute(product_block, ALL, [(b, a) for a, b in pairs])]
    all_to_all x2 -> x3, starting transfers between devices: 23.9 us -> 20.5 us  [exchange(): return lax.all_to_all(value, axis, 0, 0, tiled=True)]
    all_gather x1, blocking collectives: 17.2 us -> 19.2 us  [shards(): gathered = lax.all_gather(jnp.concatenate([back, packed], 0), COLS, axis=0)]
  transfers between devices with their start and end apart: 4 -> 5, of which waited for: 3 -> 3; matrix products, arithmetic and copies ran while one was open for 3% -> 1% of each run, Pallas kernels for 0% -> 0%
where the time goes in v3:
time: 180 us; the launch traced here: 179 us
  blocking collectives  79.4 us (44%)
  waiting for transfers between devices  44.4 us (25%)
  starting transfers between devices  29.5 us (16%)
  Pallas kernels  12.8 us (7%)
  matrix products  9.48 us (5%)
  local copies, waits for them, and re-layouts  2.01 us (1%)
    all_to_all x3, blocking collectives, exchange(): return lax.all_to_all(value, axis, 0, 0, tiled=True)  37.5 us
    all_to_all x3, waiting for transfers between devices, exchange(): return lax.all_to_all(value, axis, 0, 0, tiled=True)  31.4 us
    all_gather x1, blocking collectives, shards(): panel_rows = lax.all_gather(panel, COLS, axis=1, tiled=True)  22.7 us
    all_to_all x3, starting transfers between devices, exchange(): return lax.all_to_all(value, axis, 0, 0, tiled=True)  20.5 us
    all_gather x1, blocking collectives, shards(): gathered = lax.all_gather(jnp.concatenate([back, packed], 0), COLS, axis=0)  19.2 us
    ppermute x1, waiting for transfers between devices, shards(): panel_block = lax.ppermute(block, ALL, pairs)  13 us
    pallas_call x1, Pallas kernels, finish(): pl.pallas_call(finish_kernel, out_shape=(jax.ShapeDtypeStruct((rows, widt...  12.8 us
    dot_general x3, matrix products, matmul(): lax.dot_general(left, right, ((contract[:1], contract[1:]), ((), ())), pr...  9.48 us
  transfers between devices with their start and end apart: 5, of which 3 were waited for; matrix products, arithmetic and copies ran while one was open for 1% of the time, Pallas kernels for 0%

profile of v3, /device:TPU:1, one launch (start us, length us, event | category | flops | bytes accessed | tf_op | source)
XLA Modules:
  0.0 179.4 jit_solution(13126234951136758882)
XLA Ops:
  0.6 22.7 %all_gather.9 = f32[512,256]{0,1:T(8,128)S(1)} all-gather(f32[512,16]{0,1:T(8,128)} %param.3), channel_id=1, replica_groups=mesh['z'=8,'x'=4,'y'=8,'c'=2] {'y','c'}, dimensions={1}, use_global_device_ids=true | all-gather | bytes 557056 | tf_op jit(solution)/shard_map/all_gather | solution.py:143
  23.3 4.4 %fusion.3 = f32[1024,256]{1,0:T(8,128)} fusion(f32[512,1024]{1,0:T(8,128)} %param.2, f32[512,256]{0,1:T(8,128)S(1)} %all_gather.9), kind=kOutput, calls=%fused_computation.19 | convolution fusion | flops 805306368 | bytes 3670016 | tf_op jit(solution)/shard_map/dot_general | solution.py:15
  27.7 3.5 %all-to-all-start = ((f32[4,256,256]{2,1,0:T(8,128)}), f32[4,256,256]{2,1,0:T(8,128)S(1)}, u32[]{:S(2)}, u32[]{:S(2)}) async-start(f32[4,256,256]{2,1,0:T(8,128)} %bitcast), calls=%async_computation | async-start | bytes 2097152 | tf_op jit(solution)/shard_map/all_to_all | solution.py:119
  31.2 0.1 constant_dynamic-slice_fusion
  31.3 3.6 %collective-permute-start = (f32[32,256]{0,1:T(8,128)S(1)}, f32[32,256]{0,1:T(8,128)S(1)}, u32[]{:S(2)}, u32[]{:S(2)}) collective-permute-start(f32[32,256]{0,1:T(8,128)S(1)} %constant_dynamic-slice_fusion), channel_id=1, source_target_pairs={{0,0},{32,1},{64,2},{96,3},{128,4},{160,5},{192,6},{224,7},{256,8}... | collective-permute-start | bytes 98312 | tf_op jit(solution)/shard_map/ppermute | solution.py:145
  35.0 13.0 %collective-permute-done = f32[32,256]{0,1:T(8,128)S(1)} collective-permute-done((f32[32,256]{0,1:T(8,128)S(1)}, f32[32,256]{0,1:T(8,128)S(1)}, u32[]{:S(2)}, u32[]{:S(2)}) %collective-permute-start) | collective-permute-done | bytes 32800 | tf_op jit(solution)/shard_map/ppermute | solution.py:145
  48.0 0.0 all-to-all-done
  48.0 0.8 reduce_sum.45
  48.7 13.4 %all-to-all-start.1 = ((f32[8,32,256]{2,1,0:T(8,128)}), f32[8,32,256]{2,1,0:T(8,128)S(1)}, u32[]{:S(2)}, u32[]{:S(2)}) async-start(f32[8,32,256]{2,1,0:T(8,128)} %bitcast.1), calls=%async_computation.1 | async-start | bytes 524288 | tf_op jit(solution)/shard_map/all_to_all | solution.py:119
  62.1 0.1 copy.13
  62.2 10.9 %all-to-all-done.1 = f32[8,32,256]{2,1,0:T(8,128)S(1)} async-done(((f32[8,32,256]{2,1,0:T(8,128)}), f32[8,32,256]{2,1,0:T(8,128)S(1)}, u32[]{:S(2)}, u32[]{:S(2)}) %all-to-all-start.1) | async-done | bytes 262176 | tf_op jit(solution)/shard_map/all_to_all | solution.py:119
  73.1 0.1 broadcast_in_dim.25
  73.1 20.5 %all_to_all.30 = f32[8,32,512]{2,1,0:T(8,128)S(1)} all-to-all(f32[8,32,512]{2,1,0:T(8,128)S(1)} %broadcast_in_dim.25), channel_id=1, replica_groups=mesh['z'=8,'x'=4,'y'=8,'c'=2] {'z'}, dimensions={0} | all-to-all | bytes 1048576 | tf_op jit(solution)/shard_map/all_to_all | solution.py:119
  93.6 1.6 broadcast_in_dim.27
  95.2 3.6 %all-to-all-start.3 = ((f32[4,256,512]{2,1,0:T(8,128)}), f32[4,256,512]{2,1,0:T(8,128)S(1)}, u32[]{:S(2)}, u32[]{:S(2)}) async-start(f32[4,256,512]{2,1,0:T(8,128)} %broadcast_in_dim.27), calls=%async_computation.3 | async-start | bytes 4194304 | tf_op jit(solution)/shard_map/all_to_all | solution.py:119
  98.8 5.4 %collective-permute-start.1 = (f32[32,256]{1,0:T(8,128)S(1)}, f32[32,256]{1,0:T(8,128)S(1)}, u32[]{:S(2)}, u32[]{:S(2)}) collective-permute-start(f32[32,256]{1,0:T(8,128)S(1)} %reduce_sum.46), channel_id=1, source_target_pairs={{0,0},{1,32},{2,64},{3,96},{4,128},{5,160},{6,192},{7,224},{8,256}... | collective-permute-start | bytes 98312 | tf_op jit(solution)/shard_map/ppermute | solution.py:157
  104.2 20.6 %all-to-all-done.3 = f32[4,256,512]{2,1,0:T(8,128)S(1)} async-done(((f32[4,256,512]{2,1,0:T(8,128)}), f32[4,256,512]{2,1,0:T(8,128)S(1)}, u32[]{:S(2)}, u32[]{:S(2)}) %all-to-all-start.3) | async-done | bytes 2097184 | tf_op jit(solution)/shard_map/all_to_all | solution.py:119
  124.8 1.9 %fusion = f32[256,512]{1,0:T(8,128)S(1)} fusion(f32[1024,512]{1,0:T(8,128)S(1)} %bitcast.16), kind=kOutput, calls=%fused_computation.1 | convolution fusion | flops 1610612736 | bytes 3670016 | tf_op jit(solution)/shard_map/dot_general | solution.py:15
  126.7 0.1 slice_select_fusion
  126.8 0.2 copy.14
  126.9 0.1 fusion.2
  127.0 0.0 collective-permute-done.1
  127.1 5.2 %all_to_all.31 = f32[2,8,17,256]{3,1,2,0:T(8,128)S(1)} all-to-all(f32[2,8,17,256]{3,1,2,0:T(8,128)S(1)} %maximum_bitcast_fusion), channel_id=1, replica_groups=mesh['z'=8,'x'=4,'y'=8,'c'=2] {'c'}, dimensions={0} | all-to-all | bytes 557056 | tf_op jit(solution)/shard_map/all_to_all | solution.py:119
  132.3 11.9 %all_to_all.32 = f32[8,17,256]{2,1,0:T(8,128)S(1)} all-to-all(f32[8,17,256]{2,1,0:T(8,128)S(1)} %copy.15), channel_id=1, replica_groups=mesh['z'=8,'x'=4,'y'=8,'c'=2] {'y'}, dimensions={0} | all-to-all | bytes 278528 | tf_op jit(solution)/shard_map/all_to_all | solution.py:119
  144.2 19.2 %all-gather.1.gathered_ref = f32[16,49,256]{2,1,0:T(8,128)S(1)} all-gather(f32[1,49,256]{2,1,0:T(8,128)S(1)} %maximum_bitcast_fusion.1), channel_id=2, replica_groups=mesh['z'=8,'x'=4,'y'=8,'c'=2] {'y','c'}, dimensions={0}, use_global_device_ids=true | all-gather | bytes 852992 | tf_op jit(solution)/shard_map/all_gather | solution.py:171
  163.4 0.0 copy-start
  163.4 12.8 %finish.1 = (f32[512,256]{1,0:T(8,128)}, f32[512,512]{1,0:T(8,128)S(1)}) custom-call(f32[16,49,256]{2,1,0:T(8,128)S(1)} %all-gather.1.gathered_ref, f32[256,512]{1,0:T(8,128)S(1)} %bitcast.15), custom_call_target="tpu_custom_call" | custom-call | flops 2000000000 | bytes 4000000 | tf_op jit(solution)/shard_map/finish/pallas_call | solution.py:102
  176.3 0.0 copy-done
  176.3 3.2 %convolution_subtract_fusion = f32[512,1024]{1,0:T(8,128)} fusion(f32[512,1024]{1,0:T(8,128)S(1)} %copy-done, f32[512,512]{1,0:T(8,128)S(1)} %get-tuple-element.12, f32[1024,512]{1,0:T(8,128)S(1)} %bitcast.17), kind=kOutput, calls=%fused_computation | convolution fusion | flops 1611137024 | bytes 7340032 | tf_op jit(solution)/shard_map/dot_general | solution.py:15
  (10 shorter events, 0.2 us)
Async XLA Ops:
  27.7 20.3 %all-to-all-start = ((f32[4,256,256]{2,1,0:T(8,128)}), f32[4,256,256]{2,1,0:T(8,128)S(1)}, u32[]{:S(2)}, u32[]{:S(2)}) async-start(f32[4,256,256]{2,1,0:T(8,128)} %bitcast), calls=%async_computation | async-start | bytes 2097152 | tf_op jit(solution)/shard_map/all_to_all | solution.py:119
  31.3 16.6 %collective-permute-start = (f32[32,256]{0,1:T(8,128)S(1)}, f32[32,256]{0,1:T(8,128)S(1)}, u32[]{:S(2)}, u32[]{:S(2)}) collective-permute-start(f32[32,256]{0,1:T(8,128)S(1)} %constant_dynamic-slice_fusion), channel_id=1, source_target_pairs={{0,0},{32,1},{64,2},{96,3},{128,4},{160,5},{192,6},{224,7},{256,8}... | collective-permute-start | bytes 98312 | tf_op jit(solution)/shard_map/ppermute | solution.py:145
  48.7 24.3 %all-to-all-start.1 = ((f32[8,32,256]{2,1,0:T(8,128)}), f32[8,32,256]{2,1,0:T(8,128)S(1)}, u32[]{:S(2)}, u32[]{:S(2)}) async-start(f32[8,32,256]{2,1,0:T(8,128)} %bitcast.1), calls=%async_computation.1 | async-start | bytes 524288 | tf_op jit(solution)/shard_map/all_to_all | solution.py:119
  95.2 29.6 %all-to-all-start.3 = ((f32[4,256,512]{2,1,0:T(8,128)}), f32[4,256,512]{2,1,0:T(8,128)S(1)}, u32[]{:S(2)}, u32[]{:S(2)}) async-start(f32[4,256,512]{2,1,0:T(8,128)} %broadcast_in_dim.27), calls=%async_computation.3 | async-start | bytes 4194304 | tf_op jit(solution)/shard_map/all_to_all | solution.py:119
  98.8 28.2 %collective-permute-start.1 = (f32[32,256]{1,0:T(8,128)S(1)}, f32[32,256]{1,0:T(8,128)S(1)}, u32[]{:S(2)}, u32[]{:S(2)}) collective-permute-start(f32[32,256]{1,0:T(8,128)S(1)} %reduce_sum.46), channel_id=1, source_target_pairs={{0,0},{1,32},{2,64},{3,96},{4,128},{5,160},{6,192},{7,224},{8,256}... | collective-permute-start | bytes 98312 | tf_op jit(solution)/shard_map/ppermute | solution.py:157
  163.4 12.8 %copy-start = (f32[512,1024]{1,0:T(8,128)S(1)}, f32[512,1024]{1,0:T(8,128)}, u32[]{:S(2)}) copy-start(f32[512,1024]{1,0:T(8,128)} %param.2) | copy-start | bytes 6291460

commit v4 on v3

--- a/solution.py
+++ b/solution.py
@@ -16,6 +16,38 @@
         left, right, ((contract[:1], contract[1:]), ((), ())),
         precision=precision, preferred_element_type=jnp.float32,
     )
+
+
+def split(value):
+    top = value.astype(jnp.bfloat16)
+    return top, (value - top.astype(jnp.float32)).astype(jnp.bfloat16)
+
+
+def matmul3(left, right, contract):
+    (a, b), (c, d) = split(left), split(right)
+    low = matmul(a, d, contract, None) + matmul(b, c, contract, None)
+    return matmul(a, c, contract, None) + low
+
+
+def partial_kernel(panel_ref, trailing_ref, out_ref):
+    out_ref[...] = matmul3(panel_ref[...], trailing_ref[...], (1, 0)).T
+
+
+def partial_product(panel, trailing):
+    (width, rows), columns = panel.shape, trailing.shape[1]
+    return pl.pallas_call(
+        partial_kernel,
+        grid=(columns // 256,),
+        in_specs=[
+            pl.BlockSpec((width, rows), lambda i: (0, 0)),
+            pl.BlockSpec((rows, 256), lambda i: (0, i)),
+        ],
+        out_specs=pl.BlockSpec((256, width), lambda i: (i, 0)),
+        out_shape=jax.ShapeDtypeStruct((columns, width), jnp.float32),
+        compiler_params=pltpu.CompilerParams(vmem_limit_bytes=60 * 2**20),
+        cost_estimate=pl.CostEstimate(flops=8 * 10**8, bytes_accessed=4 * 10**6, transcendentals=0),
+        name="partial_product",
+    )(panel, trailing)
 
 
 def iota(shape, dimension):
@@ -144,7 +176,7 @@
     block = lax.dynamic_slice(panel_rows, (place * BLOCK, 0), (BLOCK, width))
     panel_block = lax.ppermute(block, ALL, pairs)
 
-    partial = matmul(trailing, panel_rows, (0, 0), high)
+    partial = partial_product(panel_rows.T, trailing)
     partial = exchange(partial.reshape(4, 256, width), "x")
     partial, panel_block = lax.optimization_barrier((partial, panel_block))
     partial = partial.sum(0)

time: 180 us -> 182 us (1.011)
  Pallas kernels: 12.8 us -> 17.5 us
  matrix products: 9.48 us -> 5.11 us
    pallas_call x0 -> x1, Pallas kernels: none -> 4.65 us  [partial_product(): pl.pallas_call(partial_kernel, grid=(columns // 256,), in_specs=[pl.Block...]
    dot_general x3 -> x2, matrix products: 9.48 us -> 5.11 us  [matmul(): lax.dot_general(left, right, ((contract[:1], contract[1:]), ((), ())), pr...]
where the time goes in v4:
time: 182 us; the launch traced here: 181 us
  blocking collectives  80.8 us (44%)
  waiting for transfers between devices  44.4 us (24%)
  starting transfers between devices  29.5 us (16%)
  Pallas kernels  17.5 us (10%)
  matrix products  5.11 us (3%)
  local copies, waits for them, and re-layouts  2.01 us (1%)
    all_to_all x3, blocking collectives, exchange(): return lax.all_to_all(value, axis, 0, 0, tiled=True)  37.5 us
    all_to_all x3, waiting for transfers between devices, exchange(): return lax.all_to_all(value, axis, 0, 0, tiled=True)  31.4 us
    all_gather x1, blocking collectives, shards(): panel_rows = lax.all_gather(panel, COLS, axis=1, tiled=True)  24.1 us
    all_to_all x3, starting transfers between devices, exchange(): return lax.all_to_all(value, axis, 0, 0, tiled=True)  20.5 us
    all_gather x1, blocking collectives, shards(): gathered = lax.all_gather(jnp.concatenate([back, packed], 0), COLS, axis=0)  19.2 us
    ppermute x1, waiting for transfers between devices, shards(): panel_block = lax.ppermute(block, ALL, pairs)  13 us
    pallas_call x1, Pallas kernels, finish(): pl.pallas_call(finish_kernel, out_shape=(jax.ShapeDtypeStruct((rows, widt...  12.8 us
    ppermute x1, starting transfers between devices, shards(): back = lax.ppermute(product_block, ALL, [(b, a) for a, b in pairs])  5.39 us
  transfers between devices with their start and end apart: 5, of which 3 were waited for; matrix products, arithmetic and copies ran while one was open for 1% of the time, Pallas kernels for 0%

profile of v4, /device:TPU:1, one launch (start us, length us, event | category | flops | bytes accessed | tf_op | source)
XLA Modules:
  0.0 181.1 jit_solution(12935656506550770144)
XLA Ops:
  0.6 24.1 %all_gather.9 = f32[512,256]{0,1:T(8,128)} all-gather(f32[512,16]{0,1:T(8,128)} %param.3), channel_id=1, replica_groups=mesh['z'=8,'x'=4,'y'=8,'c'=2] {'y','c'}, dimensions={1}, use_global_device_ids=true | all-gather | bytes 557056 | tf_op jit(solution)/shard_map/all_gather | solution.py:175
  24.7 0.0 copy-start
  24.7 4.7 %partial_product.1 = f32[1024,256]{1,0:T(8,128)} custom-call(f32[256,512]{1,0:T(8,128)} %bitcast.13, f32[512,1024]{1,0:T(8,128)} %trailing_ref.1), custom_call_target="tpu_custom_call" | custom-call | flops 800000000 | bytes 4000000 | tf_op jit(solution)/shard_map/partial_product/pallas_call | solution.py:38
  29.4 3.5 %all-to-all-start = ((f32[4,256,256]{2,1,0:T(8,128)}), f32[4,256,256]{2,1,0:T(8,128)S(1)}, u32[]{:S(2)}, u32[]{:S(2)}) async-start(f32[4,256,256]{2,1,0:T(8,128)} %bitcast.17), calls=%async_computation | async-start | bytes 2097152 | tf_op jit(solution)/shard_map/all_to_all | solution.py:151
  32.9 0.0 copy-done
  32.9 0.1 constant_dynamic-slice_fusion
  33.0 3.6 %collective-permute-start = (f32[32,256]{0,1:T(8,128)S(1)}, f32[32,256]{0,1:T(8,128)S(1)}, u32[]{:S(2)}, u32[]{:S(2)}) collective-permute-start(f32[32,256]{0,1:T(8,128)S(1)} %constant_dynamic-slice_fusion), channel_id=1, source_target_pairs={{0,0},{32,1},{64,2},{96,3},{128,4},{160,5},{192,6},{224,7},{256,8}... | collective-permute-start | bytes 98312 | tf_op jit(solution)/shard_map/ppermute | solution.py:177
  36.7 13.0 %collective-permute-done = f32[32,256]{0,1:T(8,128)S(1)} collective-permute-done((f32[32,256]{0,1:T(8,128)S(1)}, f32[32,256]{0,1:T(8,128)S(1)}, u32[]{:S(2)}, u32[]{:S(2)}) %collective-permute-start) | collective-permute-done | bytes 32800 | tf_op jit(solution)/shard_map/ppermute | solution.py:177
  49.6 0.0 all-to-all-done
  49.6 0.8 reduce_sum.45
  50.4 13.4 %all-to-all-start.1 = ((f32[8,32,256]{2,1,0:T(8,128)}), f32[8,32,256]{2,1,0:T(8,128)S(1)}, u32[]{:S(2)}, u32[]{:S(2)}) async-start(f32[8,32,256]{2,1,0:T(8,128)} %bitcast.2), calls=%async_computation.1 | async-start | bytes 524288 | tf_op jit(solution)/shard_map/all_to_all | solution.py:151
  63.8 0.1 copy.13
  63.8 10.9 %all-to-all-done.1 = f32[8,32,256]{2,1,0:T(8,128)S(1)} async-done(((f32[8,32,256]{2,1,0:T(8,128)}), f32[8,32,256]{2,1,0:T(8,128)S(1)}, u32[]{:S(2)}, u32[]{:S(2)}) %all-to-all-start.1) | async-done | bytes 262176 | tf_op jit(solution)/shard_map/all_to_all | solution.py:151
  74.7 0.1 broadcast_in_dim.25
  74.8 20.5 %all_to_all.30 = f32[8,32,512]{2,1,0:T(8,128)S(1)} all-to-all(f32[8,32,512]{2,1,0:T(8,128)S(1)} %broadcast_in_dim.25), channel_id=1, replica_groups=mesh['z'=8,'x'=4,'y'=8,'c'=2] {'z'}, dimensions={0} | all-to-all | bytes 1048576 | tf_op jit(solution)/shard_map/all_to_all | solution.py:151
  95.2 1.6 broadcast_in_dim.27
  96.8 3.6 %all-to-all-start.3 = ((f32[4,256,512]{2,1,0:T(8,128)}), f32[4,256,512]{2,1,0:T(8,128)S(1)}, u32[]{:S(2)}, u32[]{:S(2)}) async-start(f32[4,256,512]{2,1,0:T(8,128)} %broadcast_in_dim.27), calls=%async_computation.3 | async-start | bytes 4194304 | tf_op jit(solution)/shard_map/all_to_all | solution.py:151
  100.5 5.4 %collective-permute-start.1 = (f32[32,256]{1,0:T(8,128)S(1)}, f32[32,256]{1,0:T(8,128)S(1)}, u32[]{:S(2)}, u32[]{:S(2)}) collective-permute-start(f32[32,256]{1,0:T(8,128)S(1)} %reduce_sum.46), channel_id=1, source_target_pairs={{0,0},{1,32},{2,64},{3,96},{4,128},{5,160},{6,192},{7,224},{8,256}... | collective-permute-start | bytes 98312 | tf_op jit(solution)/shard_map/ppermute | solution.py:189
  105.9 20.6 %all-to-all-done.3 = f32[4,256,512]{2,1,0:T(8,128)S(1)} async-done(((f32[4,256,512]{2,1,0:T(8,128)}), f32[4,256,512]{2,1,0:T(8,128)S(1)}, u32[]{:S(2)}, u32[]{:S(2)}) %all-to-all-start.3) | async-done | bytes 2097184 | tf_op jit(solution)/shard_map/all_to_all | solution.py:151
  126.5 1.9 %fusion = f32[256,512]{1,0:T(8,128)S(1)} fusion(f32[1024,512]{1,0:T(8,128)S(1)} %bitcast.15), kind=kOutput, calls=%fused_computation.1 | convolution fusion | flops 1610612736 | bytes 3670016 | tf_op jit(solution)/shard_map/dot_general | solution.py:15
  128.4 0.1 slice_select_fusion
  128.5 0.2 copy.14
  128.6 0.1 fusion.2
  128.7 0.0 collective-permute-done.1
  128.7 5.2 %all_to_all.31 = f32[2,8,17,256]{3,1,2,0:T(8,128)S(1)} all-to-all(f32[2,8,17,256]{3,1,2,0:T(8,128)S(1)} %maximum_bitcast_fusion), channel_id=1, replica_groups=mesh['z'=8,'x'=4,'y'=8,'c'=2] {'c'}, dimensions={0} | all-to-all | bytes 557056 | tf_op jit(solution)/shard_map/all_to_all | solution.py:151
  134.0 11.9 %all_to_all.32 = f32[8,17,256]{2,1,0:T(8,128)S(1)} all-to-all(f32[8,17,256]{2,1,0:T(8,128)S(1)} %copy.15), channel_id=1, replica_groups=mesh['z'=8,'x'=4,'y'=8,'c'=2] {'y'}, dimensions={0} | all-to-all | bytes 278528 | tf_op jit(solution)/shard_map/all_to_all | solution.py:151
  145.9 19.2 %all-gather.1.gathered_ref = f32[16,49,256]{2,1,0:T(8,128)S(1)} all-gather(f32[1,49,256]{2,1,0:T(8,128)S(1)} %maximum_bitcast_fusion.1), channel_id=2, replica_groups=mesh['z'=8,'x'=4,'y'=8,'c'=2] {'y','c'}, dimensions={0}, use_global_device_ids=true | all-gather | bytes 852992 | tf_op jit(solution)/shard_map/all_gather | solution.py:203
  165.1 0.0 copy-start.1
  165.1 12.8 %finish.1 = (f32[512,256]{1,0:T(8,128)}, f32[512,512]{1,0:T(8,128)S(1)}) custom-call(f32[16,49,256]{2,1,0:T(8,128)S(1)} %all-gather.1.gathered_ref, f32[256,512]{1,0:T(8,128)S(1)} %bitcast.14), custom_call_target="tpu_custom_call" | custom-call | flops 2000000000 | bytes 4000000 | tf_op jit(solution)/shard_map/finish/pallas_call | solution.py:134
  177.9 0.0 copy-done.1
  177.9 3.2 %convolution_subtract_fusion = f32[512,1024]{1,0:T(8,128)} fusion(f32[512,1024]{1,0:T(8,128)S(1)} %copy-done.1, f32[512,512]{1,0:T(8,128)S(1)} %get-tuple-element.12, f32[1024,512]{1,0:T(8,128)S(1)} %bitcast.16), kind=kOutput, calls=%fused_computation | convolution fusion | flops 1611137024 | bytes 7340032 | tf_op jit(solution)/shard_map/dot_general | solution.py:15
  (10 shorter events, 0.2 us)
Async XLA Ops:
  24.7 8.2 %copy-start = (f32[512,256]{0,1:T(8,128)S(1)}, f32[512,256]{0,1:T(8,128)}, u32[]{:S(2)}) copy-start(f32[512,256]{0,1:T(8,128)} %all_gather.9) | copy-start | bytes 1572868
  29.4 20.3 %all-to-all-start = ((f32[4,256,256]{2,1,0:T(8,128)}), f32[4,256,256]{2,1,0:T(8,128)S(1)}, u32[]{:S(2)}, u32[]{:S(2)}) async-start(f32[4,256,256]{2,1,0:T(8,128)} %bitcast.17), calls=%async_computation | async-start | bytes 2097152 | tf_op jit(solution)/shard_map/all_to_all | solution.py:151
  33.0 16.6 %collective-permute-start = (f32[32,256]{0,1:T(8,128)S(1)}, f32[32,256]{0,1:T(8,128)S(1)}, u32[]{:S(2)}, u32[]{:S(2)}) collective-permute-start(f32[32,256]{0,1:T(8,128)S(1)} %constant_dynamic-slice_fusion), channel_id=1, source_target_pairs={{0,0},{32,1},{64,2},{96,3},{128,4},{160,5},{192,6},{224,7},{256,8}... | collective-permute-start | bytes 98312 | tf_op jit(solution)/shard_map/ppermute | solution.py:177
  50.4 24.3 %all-to-all-start.1 = ((f32[8,32,256]{2,1,0:T(8,128)}), f32[8,32,256]{2,1,0:T(8,128)S(1)}, u32[]{:S(2)}, u32[]{:S(2)}) async-start(f32[8,32,256]{2,1,0:T(8,128)} %bitcast.2), calls=%async_computation.1 | async-start | bytes 524288 | tf_op jit(solution)/shard_map/all_to_all | solution.py:151
  96.8 29.6 %all-to-all-start.3 = ((f32[4,256,512]{2,1,0:T(8,128)}), f32[4,256,512]{2,1,0:T(8,128)S(1)}, u32[]{:S(2)}, u32[]{:S(2)}) async-start(f32[4,256,512]{2,1,0:T(8,128)} %broadcast_in_dim.27), calls=%async_computation.3 | async-start | bytes 4194304 | tf_op jit(solution)/shard_map/all_to_all | solution.py:151
  100.5 28.2 %collective-permute-start.1 = (f32[32,256]{1,0:T(8,128)S(1)}, f32[32,256]{1,0:T(8,128)S(1)}, u32[]{:S(2)}, u32[]{:S(2)}) collective-permute-start(f32[32,256]{1,0:T(8,128)S(1)} %reduce_sum.46), channel_id=1, source_target_pairs={{0,0},{1,32},{2,64},{3,96},{4,128},{5,160},{6,192},{7,224},{8,256}... | collective-permute-start | bytes 98312 | tf_op jit(solution)/shard_map/ppermute | solution.py:189
  165.1 12.8 %copy-start.1 = (f32[512,1024]{1,0:T(8,128)S(1)}, f32[512,1024]{1,0:T(8,128)}, u32[]{:S(2)}) copy-start(f32[512,1024]{1,0:T(8,128)} %trailing_ref.1) | copy-start | bytes 6291460
